TPU v7x, 32 devices: a whole 2x2x4 slice. The times are simulated.
32 devices in a mesh: parts: 2 (over x), row: 16 (over z, y, core).
Axes of the slice: x: 2, y: 2, z: 4, core: 2. Of those that a mesh axis runs over, the one named last changes fastest.
Arguments:
- solid_points: float32 [768, 3, 256], P(('parts', 'row')), parts along dimension 0
- solid_counts: int32 [768], P(('parts', 'row')), parts along dimension 0, may hold values from 64 to 256, as said below
- fluid_points: float32 [1536, 3, 256], P(('parts', 'row')), parts along dimension 0
- fluid_forces: float32 [1536, 3, 256], P(('parts', 'row')), parts along dimension 0
- fluid_counts: int32 [1536], P(('parts', 'row')), parts along dimension 0, may hold values from 64 to 256, as said below
- ss_pairs: int32 [768, 9], P(('parts', 'row')), parts along dimension 0, may hold values from -1 to 383, as said below
- sf_pairs: int32 [768, 18], P(('parts', 'row')), parts along dimension 0, may hold values from -1 to 767, as said below
Outputs:
- mapped_forces: float32 [768, 3, 256], P(('parts', 'row')), parts along dimension 0
- residual: float32 [768, 3, 256], P(('parts', 'row')), parts along dimension 0
There are 2 independent parts, one for each index of `parts`. A program takes and returns all parts, laid end to end along the dimension named above; each array names one. Nothing has to cross between parts.
Inputs may be any that keep to these rules, and one draw needn't show every extreme that they name: The first solid_counts[b] vertex slots of box b hold its vertices; the others are padding. The first fluid_counts[f] vertex slots of box f hold its vertices; the others are padding. `ss_pairs`: row b begins with b itself, then solid boxes paired with b, each between b - 24 and b + 24 and none twice, in some order, then -1 in the unused slots. Box e is listed in row b exactly when b is listed in row e. Some row has all 9 slots live. `sf_pairs`: row b begins with 2 b and 2 b + 1, then other fluid boxes paired with solid box b, each between 2 b - 48 and 2 b + 2 * 24 + 1 and none twice, in some order, then -1 in the unused slots. Some row has all 18 slots live.
All inputs are finite; a program needn't handle non-finite values.
Results may differ from a plain program's by a relative error of at most 0.0003.
Values sent between devices are 32-bit elements; how exact they have to be, the bound alone decides.
A program may use at most 64 MiB of HBM per device.

v0:
```python
import math

import jax
import jax.numpy as jnp
from jax import lax
from jax.sharding import PartitionSpec as P

ITERS = 2


RADIUS = 0.9
DIAGONAL_SHIFT = 0.5
GROUP_SLOTS = 3


def with_halo(block, sides, width):
    for axis, dim in sides:
        count = lax.axis_size(axis)
        forward = [(i, i + 1) for i in range(count - 1)]
        backward = [(target, source) for source, target in forward]
        low = lax.ppermute(
            lax.slice_in_dim(block, block.shape[dim] - width, None, axis=dim), axis, forward
        )
        high = lax.ppermute(lax.slice_in_dim(block, 0, width, axis=dim), axis, backward)
        block = jnp.concatenate([low, block, high], axis=dim)
    return block


def wendland(squared):
    scaled = jnp.sqrt(squared) / RADIUS
    falling = jnp.maximum(1.0 - scaled, 0.0)
    return falling * falling * falling * falling * (4.0 * scaled + 1.0)


def group_distances(points, nearby):
    along_x = points[:, None, 0, :, None] - nearby[:, :, 0, None, :]
    along_y = points[:, None, 1, :, None] - nearby[:, :, 1, None, :]
    along_z = points[:, None, 2, :, None] - nearby[:, :, 2, None, :]
    return along_x * along_x + along_y * along_y + along_z * along_z


def pair_terms(points, others, values, pair_ids, offset, slot_limit):
    box_total = pair_ids.shape[0]
    filler = jnp.full((box_total, GROUP_SLOTS), -1, jnp.int32)
    padded_ids = jnp.concatenate([pair_ids, filler], axis=1)
    group_total = (slot_limit + GROUP_SLOTS - 1) // GROUP_SLOTS

    def add_group(group_index, running):
        columns = lax.dynamic_slice_in_dim(padded_ids, group_index * GROUP_SLOTS, GROUP_SLOTS, 1)
        live_mask = columns >= 0
        position = jnp.where(live_mask, columns - offset, 0)
        nearby = jnp.take(others, position, axis=0)
        carried = jnp.where(live_mask[:, :, None, None], jnp.take(values, position, axis=0), 0.0)
        kernel = wendland(group_distances(points, nearby))
        return running + jnp.einsum(
            "sgij,sgcj->sci", kernel, carried, precision=lax.Precision.HIGHEST
        )

    zeros_init = jnp.zeros((points.shape[0], 3, points.shape[2]), jnp.float32)
    return lax.fori_loop(0, group_total, add_group, zeros_init)


def lane_mask(counts, box_width):
    lane_ids = jnp.arange(box_width, dtype=jnp.int32)
    return (lane_ids[None, :] < counts[:, None]).astype(jnp.float32)[:, None, :]


def per_component(first_field, second_field):
    return jnp.sum(first_field * second_field, axis=(0, 2))


def expand(factor):
    return factor[None, :, None]


def body(solid_points, solid_counts, fluid_points, fluid_forces, fluid_counts, ss_pairs, sf_pairs):
    box_count = solid_points.shape[0]
    box_width = solid_points.shape[2]
    fluid_count = fluid_points.shape[0]
    row_index = lax.axis_index("row")
    solid_mask = lane_mask(solid_counts, box_width)
    fluid_loads = fluid_forces * lane_mask(fluid_counts, box_width)
    beside_all = with_halo(solid_points, (("row", 0),), box_count)
    packed = jnp.concatenate([fluid_points, fluid_loads], axis=1)
    fluid_ext = with_halo(packed, (("row", 0),), fluid_count)
    first_fluid = row_index * fluid_count - fluid_count
    mapped = pair_terms(
        solid_points, fluid_ext[:, 0:3], fluid_ext[:, 3:6], sf_pairs, first_fluid, sf_pairs.shape[1]
    )
    right_side = solid_mask * (mapped * (1.0 / math.sqrt(box_width)))
    first_solid = row_index * box_count - box_count

    def squared_norm(field):
        return lax.psum(per_component(field, field), "row")

    solution = jnp.zeros_like(right_side)
    residual = right_side
    direction = right_side
    norm_now = squared_norm(residual)
    for iteration in range(ITERS):
        spread = with_halo(direction, (("row", 0),), box_count)
        image = pair_terms(
            solid_points, beside_all, spread, ss_pairs, first_solid, ss_pairs.shape[1]
        )
        image = solid_mask * (image / box_width) + DIAGONAL_SHIFT * direction
        curvature_now = lax.psum(per_component(direction, image), "row")
        step_size = expand(norm_now / curvature_now)
        solution = solution + step_size * direction
        residual = residual - step_size * image
        if iteration + 1 < ITERS:
            norm_next = squared_norm(residual)
            direction = residual + expand(norm_next / norm_now) * direction
            norm_now = norm_next
    return (solution, residual)


def solution(mesh):
    return jax.shard_map(
        body,
        mesh=mesh,
        in_specs=(
            P(("parts", "row"), None, None),
            P(("parts", "row")),
            P(("parts", "row"), None, None),
            P(("parts", "row"), None, None),
            P(("parts", "row")),
            P(("parts", "row"), None),
            P(("parts", "row"), None),
        ),
        out_specs=(P(("parts", "row"), None, None), P(("parts", "row"), None, None)),
        check_vma=False,
    )
```

profile of v0, /device:TPU:3, one launch (start us, length us, event | category | flops | bytes accessed | tf_op | source)
XLA Modules:
  0.0 508.6 jit_solution(10855601279539666616)
XLA Ops:
  3.6 3.7 collective-permute-start
  9.3 3.6 collective-permute-start.4
  18.2 192.7 %while.48 = (s32[]{:T(128)}, f32[24,3,256]{2,1,0:T(4,128)S(1)}, s32[24,21]{1,0:T(8,128)S(1)}, s32[]{:T(128)}, f32[144,3,256]{2,1,0:T(4,128)S(1)}, /*index=5*/f32...) while((s32[]{:T(128)}, f32[24,3,256]{2,1,0:T(4,128)S(1)}, ...), condition=%wide.region_1.0_spmd.clone, body=%wide.region_0.2_spmd.clone.sunk | while | flops 250289808 | bytes 2587125 | solution.py:60
  20.1 30.2 %fusion.139 = f32[24,3,256]{2,1,0:T(4,128)S(1)} fusion(f32[24,3,256]{2,1,0:T(4,128)S(1)} %get-tuple-element.874, f32[24,256]{1,0:T(8,128)S(1)} %get-tuple-element.875, f32[24,3,256]{2,1,0:T(4,128)S(1)} %get-tuple-element.876, f32[24,256]{1,0:T(8,128)S(1)} %get-tuple-element.877, f32[24,3,256]{2,1,0:T(4,128)S(1)} %get-tuple-element.878, ...), kind=kOutput, calls=%fused_computation.34.clone.1 | convolution fusion | flops 250232832 | bytes 663697 | tf_op jit(solution)/shard_map/while/body/eval_jaxpr/sgij,sgcj->sci/dot_general | solution.py:55
  52.2 30.2 %fusion.139 = f32[24,3,256]{2,1,0:T(4,128)S(1)} fusion(f32[24,3,256]{2,1,0:T(4,128)S(1)} %get-tuple-element.874, f32[24,256]{1,0:T(8,128)S(1)} %get-tuple-element.875, f32[24,3,256]{2,1,0:T(4,128)S(1)} %get-tuple-element.876, f32[24,256]{1,0:T(8,128)S(1)} %get-tuple-element.877, f32[24,3,256]{2,1,0:T(4,128)S(1)} %get-tuple-element.878, ...), kind=kOutput, calls=%fused_computation.34.clone.1 | convolution fusion | flops 250232832 | bytes 663697 | tf_op jit(solution)/shard_map/while/body/eval_jaxpr/sgij,sgcj->sci/dot_general | solution.py:55
  84.3 30.2 %fusion.139 = f32[24,3,256]{2,1,0:T(4,128)S(1)} fusion(f32[24,3,256]{2,1,0:T(4,128)S(1)} %get-tuple-element.874, f32[24,256]{1,0:T(8,128)S(1)} %get-tuple-element.875, f32[24,3,256]{2,1,0:T(4,128)S(1)} %get-tuple-element.876, f32[24,256]{1,0:T(8,128)S(1)} %get-tuple-element.877, f32[24,3,256]{2,1,0:T(4,128)S(1)} %get-tuple-element.878, ...), kind=kOutput, calls=%fused_computation.34.clone.1 | convolution fusion | flops 250232832 | bytes 663697 | tf_op jit(solution)/shard_map/while/body/eval_jaxpr/sgij,sgcj->sci/dot_general | solution.py:55
  116.5 30.2 %fusion.139 = f32[24,3,256]{2,1,0:T(4,128)S(1)} fusion(f32[24,3,256]{2,1,0:T(4,128)S(1)} %get-tuple-element.874, f32[24,256]{1,0:T(8,128)S(1)} %get-tuple-element.875, f32[24,3,256]{2,1,0:T(4,128)S(1)} %get-tuple-element.876, f32[24,256]{1,0:T(8,128)S(1)} %get-tuple-element.877, f32[24,3,256]{2,1,0:T(4,128)S(1)} %get-tuple-element.878, ...), kind=kOutput, calls=%fused_computation.34.clone.1 | convolution fusion | flops 250232832 | bytes 663697 | tf_op jit(solution)/shard_map/while/body/eval_jaxpr/sgij,sgcj->sci/dot_general | solution.py:55
  148.6 30.2 %fusion.139 = f32[24,3,256]{2,1,0:T(4,128)S(1)} fusion(f32[24,3,256]{2,1,0:T(4,128)S(1)} %get-tuple-element.874, f32[24,256]{1,0:T(8,128)S(1)} %get-tuple-element.875, f32[24,3,256]{2,1,0:T(4,128)S(1)} %get-tuple-element.876, f32[24,256]{1,0:T(8,128)S(1)} %get-tuple-element.877, f32[24,3,256]{2,1,0:T(4,128)S(1)} %get-tuple-element.878, ...), kind=kOutput, calls=%fused_computation.34.clone.1 | convolution fusion | flops 250232832 | bytes 663697 | tf_op jit(solution)/shard_map/while/body/eval_jaxpr/sgij,sgcj->sci/dot_general | solution.py:55
  180.7 30.2 %fusion.139 = f32[24,3,256]{2,1,0:T(4,128)S(1)} fusion(f32[24,3,256]{2,1,0:T(4,128)S(1)} %get-tuple-element.874, f32[24,256]{1,0:T(8,128)S(1)} %get-tuple-element.875, f32[24,3,256]{2,1,0:T(4,128)S(1)} %get-tuple-element.876, f32[24,256]{1,0:T(8,128)S(1)} %get-tuple-element.877, f32[24,3,256]{2,1,0:T(4,128)S(1)} %get-tuple-element.878, ...), kind=kOutput, calls=%fused_computation.34.clone.1 | convolution fusion | flops 250232832 | bytes 663697 | tf_op jit(solution)/shard_map/while/body/eval_jaxpr/sgij,sgcj->sci/dot_general | solution.py:55
  210.9 4.4 collective-permute-start.2
  217.3 3.7 collective-permute-done.3
  221.1 96.3 %while.49 = (s32[]{:T(128)}, f32[24,3,256]{2,1,0:T(4,128)S(1)}, s32[24,12]{1,0:T(8,128)S(1)}, s32[]{:T(128)}, f32[72,3,256]{2,1,0:T(4,128)S(1)}, /*index=5*/f32[...) while((s32[]{:T(128)}, f32[24,3,256]{2,1,0:T(4,128)S(1)}, ...), condition=%wide.region_5.8_spmd.clone, body=%wide.region_4.7_spmd.clone.sunk | while | flops 250289808 | bytes 2587125 | solution.py:60
  223.1 30.2 %fusion.141 = f32[24,3,256]{2,1,0:T(4,128)S(1)} fusion(f32[24,3,256]{2,1,0:T(4,128)S(1)} %get-tuple-element.890, f32[24,256]{1,0:T(8,128)S(1)} %get-tuple-element.891, f32[24,3,256]{2,1,0:T(4,128)S(1)} %get-tuple-element.892, f32[24,256]{1,0:T(8,128)S(1)} %get-tuple-element.893, f32[24,3,256]{2,1,0:T(4,128)S(1)} %get-tuple-element.894, ...), kind=kOutput, calls=%fused_computation.84.clone.1 | convolution fusion | flops 250232832 | bytes 663697 | tf_op jit(solution)/shard_map/while/body/eval_jaxpr/sgij,sgcj->sci/dot_general | solution.py:55
  255.2 30.2 %fusion.141 = f32[24,3,256]{2,1,0:T(4,128)S(1)} fusion(f32[24,3,256]{2,1,0:T(4,128)S(1)} %get-tuple-element.890, f32[24,256]{1,0:T(8,128)S(1)} %get-tuple-element.891, f32[24,3,256]{2,1,0:T(4,128)S(1)} %get-tuple-element.892, f32[24,256]{1,0:T(8,128)S(1)} %get-tuple-element.893, f32[24,3,256]{2,1,0:T(4,128)S(1)} %get-tuple-element.894, ...), kind=kOutput, calls=%fused_computation.84.clone.1 | convolution fusion | flops 250232832 | bytes 663697 | tf_op jit(solution)/shard_map/while/body/eval_jaxpr/sgij,sgcj->sci/dot_general | solution.py:55
  287.3 30.2 %fusion.141 = f32[24,3,256]{2,1,0:T(4,128)S(1)} fusion(f32[24,3,256]{2,1,0:T(4,128)S(1)} %get-tuple-element.890, f32[24,256]{1,0:T(8,128)S(1)} %get-tuple-element.891, f32[24,3,256]{2,1,0:T(4,128)S(1)} %get-tuple-element.892, f32[24,256]{1,0:T(8,128)S(1)} %get-tuple-element.893, f32[24,3,256]{2,1,0:T(4,128)S(1)} %get-tuple-element.894, ...), kind=kOutput, calls=%fused_computation.84.clone.1 | convolution fusion | flops 250232832 | bytes 663697 | tf_op jit(solution)/shard_map/while/body/eval_jaxpr/sgij,sgcj->sci/dot_general | solution.py:55
  317.6 26.5 %all-reduce.2 = (f32[3]{0:T(128)S(1)}, f32[3]{0:T(128)S(1)}) all-reduce(f32[3]{0:T(128)S(1)} %get-tuple-element.650, f32[3]{0:T(128)S(1)} %get-tuple-element.649), channel_id=1, replica_groups=mesh['parts'=2,'row'=16] {'row'}, use_global_device_ids=true, to_apply=%region_3.5 | all-reduce | flops 6 | bytes 48 | tf_op jit(solution)/shard_map/psum | solution.py:94
  344.3 32.4 %psum.30 = f32[3]{0:T(128)S(1)} all-reduce(f32[3]{0:T(128)S(1)} %get-tuple-element.704), channel_id=1, replica_groups=mesh['parts'=2,'row'=16] {'row'}, use_global_device_ids=true, to_apply=%region_9.12 | all-reduce | flops 3 | bytes 24 | tf_op jit(solution)/shard_map/psum | solution.py:94
  378.7 2.6 collective-permute-start.7
  381.3 3.1 collective-permute-done.7
  384.5 96.3 %while.50 = (s32[]{:T(128)}, f32[24,3,256]{2,1,0:T(4,128)S(1)}, s32[24,12]{1,0:T(8,128)S(1)}, s32[]{:T(128)}, f32[72,3,256]{2,1,0:T(4,128)S(1)}, /*index=5*/f32[...) while((s32[]{:T(128)}, f32[24,3,256]{2,1,0:T(4,128)S(1)}, ...), condition=%wide.region_11.14_spmd.clone, body=%wide.region_10.13_spmd.clone.sunk | while | flops 250289808 | bytes 2587125 | solution.py:60
  386.4 30.2 %fusion.143 = f32[24,3,256]{2,1,0:T(4,128)S(1)} fusion(f32[24,3,256]{2,1,0:T(4,128)S(1)} %get-tuple-element.906, f32[24,256]{1,0:T(8,128)S(1)} %get-tuple-element.907, f32[24,3,256]{2,1,0:T(4,128)S(1)} %get-tuple-element.908, f32[24,256]{1,0:T(8,128)S(1)} %get-tuple-element.909, f32[24,3,256]{2,1,0:T(4,128)S(1)} %get-tuple-element.910, ...), kind=kOutput, calls=%fused_computation.134.clone.1 | convolution fusion | flops 250232832 | bytes 663697 | tf_op jit(solution)/shard_map/while/body/eval_jaxpr/sgij,sgcj->sci/dot_general | solution.py:55
  418.5 30.2 %fusion.143 = f32[24,3,256]{2,1,0:T(4,128)S(1)} fusion(f32[24,3,256]{2,1,0:T(4,128)S(1)} %get-tuple-element.906, f32[24,256]{1,0:T(8,128)S(1)} %get-tuple-element.907, f32[24,3,256]{2,1,0:T(4,128)S(1)} %get-tuple-element.908, f32[24,256]{1,0:T(8,128)S(1)} %get-tuple-element.909, f32[24,3,256]{2,1,0:T(4,128)S(1)} %get-tuple-element.910, ...), kind=kOutput, calls=%fused_computation.134.clone.1 | convolution fusion | flops 250232832 | bytes 663697 | tf_op jit(solution)/shard_map/while/body/eval_jaxpr/sgij,sgcj->sci/dot_general | solution.py:55
  450.6 30.2 %fusion.143 = f32[24,3,256]{2,1,0:T(4,128)S(1)} fusion(f32[24,3,256]{2,1,0:T(4,128)S(1)} %get-tuple-element.906, f32[24,256]{1,0:T(8,128)S(1)} %get-tuple-element.907, f32[24,3,256]{2,1,0:T(4,128)S(1)} %get-tuple-element.908, f32[24,256]{1,0:T(8,128)S(1)} %get-tuple-element.909, f32[24,3,256]{2,1,0:T(4,128)S(1)} %get-tuple-element.910, ...), kind=kOutput, calls=%fused_computation.134.clone.1 | convolution fusion | flops 250232832 | bytes 663697 | tf_op jit(solution)/shard_map/while/body/eval_jaxpr/sgij,sgcj->sci/dot_general | solution.py:55
  481.0 26.8 %psum.31 = f32[3]{0:T(128)S(1)} all-reduce(f32[3]{0:T(128)S(1)} %multiply_reduce_fusion), channel_id=1, replica_groups=mesh['parts'=2,'row'=16] {'row'}, use_global_device_ids=true, to_apply=%region_13.16 | all-reduce | flops 3 | bytes 24 | tf_op jit(solution)/shard_map/psum | solution.py:106
  (146 shorter events, 37.9 us)
Async XLA Ops:
  0.6 8.6 %copy-start = (f32[24,3,256]{2,0,1:T(8,128)S(1)}, f32[24,3,256]{2,0,1:T(8,128)}, u32[]{:S(2)}) copy-start(f32[24,3,256]{2,0,1:T(8,128)} %param.17) | copy-start | bytes 221188
  0.6 14.2 %copy-start.4 = (s32[24]{0:T(128)S(1)}, s32[24]{0:T(128)}, u32[]{:S(2)}) copy-start(s32[24]{0:T(128)} %param.18) | copy-start | bytes 292
  0.7 14.9 %copy-start.3 = (s32[24,9]{0,1:T(8,128)S(1)}, s32[24,9]{0,1:T(8,128)}, u32[]{:S(2)}) copy-start(s32[24,9]{0,1:T(8,128)} %param.22) | copy-start | bytes 2596
  0.7 15.0 %copy-start.2 = (s32[24,18]{1,0:T(8,128)S(1)}, s32[24,18]{1,0:T(8,128)}, u32[]{:S(2)}) copy-start(s32[24,18]{1,0:T(8,128)} %param.23) | copy-start | bytes 5188
  3.6 14.2 %collective-permute-start = (f32[48,6,256]{2,1,0:T(8,128)S(1)}, f32[48,6,256]{2,1,0:T(8,128)S(1)}, u32[]{:S(2)}, u32[]{:S(2)}) collective-permute-start(f32[48,6,256]{2,1,0:T(8,128)S(1)} %pad_maximum_fusion.1), channel_id=1, source_target_pairs={{0,1},{1,2},{2,3},{3,4},{4,5},{5,6},{6,7},{7,8},{8,9},{9,10},{10,1... | collective-permute-start | bytes 884744 | tf_op jit(solution)/shard_map/ppermute | solution.py:21
  7.3 10.5 %collective-permute-start.1 = (f32[48,6,256]{2,1,0:T(8,128)S(1)}, f32[48,6,256]{2,1,0:T(8,128)S(1)}, u32[]{:S(2)}, u32[]{:S(2)}) collective-permute-start(f32[48,6,256]{2,1,0:T(8,128)S(1)} %pad_maximum_fusion.1), channel_id=1, source_target_pairs={{1,0},{2,1},{3,2},{4,3},{5,4},{6,5},{7,6},{8,7},{9,8},{10,9},{11,1... | collective-permute-start | bytes 884744 | tf_op jit(solution)/shard_map/ppermute | solution.py:24
  9.3 8.4 %collective-permute-start.4 = (f32[24,3,256]{2,1,0:T(4,128)S(1)}, f32[24,3,256]{2,1,0:T(4,128)S(1)}, u32[]{:S(2)}, u32[]{:S(2)}) collective-permute-start(f32[24,3,256]{2,1,0:T(4,128)S(1)} %copy.68), channel_id=1, source_target_pairs={{0,1},{1,2},{2,3},{3,4},{4,5},{5,6},{6,7},{7,8},{8,9},{9,10},{10,1... | collective-permute-start | bytes 221192 | tf_op jit(solution)/shard_map/ppermute | solution.py:21
  12.9 204.3 %collective-permute-start.5 = (f32[24,3,256]{2,1,0:T(4,128)S(1)}, f32[24,3,256]{2,1,0:T(4,128)S(1)}, u32[]{:S(2)}, u32[]{:S(2)}) collective-permute-start(f32[24,3,256]{2,1,0:T(4,128)S(1)} %copy.68), channel_id=1, source_target_pairs={{1,0},{2,1},{3,2},{4,3},{5,4},{6,5},{7,6},{8,7},{9,8},{10,9},{11,1... | collective-permute-start | bytes 221192 | tf_op jit(solution)/shard_map/ppermute | solution.py:24
  210.9 6.4 %collective-permute-start.2 = (f32[24,3,256]{2,0,1:T(8,128)S(1)}, f32[24,3,256]{2,0,1:T(8,128)S(1)}, u32[]{:S(2)}, u32[]{:S(2)}) collective-permute-start(f32[24,3,256]{2,0,1:T(8,128)S(1)} %copy_multiply_fusion.3), channel_id=1, source_target_pairs={{0,1},{1,2},{2,3},{3,4},{4,5},{5,6},{6,7},{7,8},{8,9},{9,10},{10,1... | collective-permute-start | bytes 221192 | tf_op jit(solution)/shard_map/ppermute | solution.py:21
  215.3 5.7 %collective-permute-start.3 = (f32[24,3,256]{2,0,1:T(8,128)S(1)}, f32[24,3,256]{2,0,1:T(8,128)S(1)}, u32[]{:S(2)}, u32[]{:S(2)}) collective-permute-start(f32[24,3,256]{2,0,1:T(8,128)S(1)} %copy_multiply_fusion.3), channel_id=1, source_target_pairs={{1,0},{2,1},{3,2},{4,3},{5,4},{6,5},{7,6},{8,7},{9,8},{10,9},{11,1... | collective-permute-start | bytes 221192 | tf_op jit(solution)/shard_map/ppermute | solution.py:24
  221.1 96.4 %copy-start.1 = (f32[24,256]{1,0:T(8,128)S(1)}, f32[24,256]{1,0:T(8,128)}, u32[]{:S(2)}) copy-start(f32[24,256]{1,0:T(8,128)} %get-tuple-element.728) | copy-start | bytes 73732
  376.8 4.5 collective-permute-start.6
  378.7 5.7 %collective-permute-start.7 = (f32[24,3,256]{2,0,1:T(8,128)S(1)}, f32[24,3,256]{2,0,1:T(8,128)S(1)}, u32[]{:S(2)}, u32[]{:S(2)}) collective-permute-start(f32[24,3,256]{2,0,1:T(8,128)S(1)} %multiply_add_fusion.1), channel_id=1, source_target_pairs={{1,0},{2,1},{3,2},{4,3},{5,4},{6,5},{7,6},{8,7},{9,8},{10,9},{11,1... | collective-permute-start | bytes 221192 | tf_op jit(solution)/shard_map/ppermute | solution.py:24
where the time goes:
time: 513 us; the launch traced here: 509 us
  matrix products  362 us (71%)
  blocking collectives  85.6 us (17%)
  starting transfers between devices  22 us (4%)
  local copies, waits for them, and re-layouts  21.3 us (4%)
  waiting for transfers between devices  8.78 us (2%)
  other arithmetic  6.87 us (1%)
    dot_general x12, matrix products, add_group(): jnp.einsum('sgij,sgcj->sci', kernel, carried, precision=lax.Precision.HIG...  362 us
    psum x2, blocking collectives, squared_norm(): return lax.psum(per_component(field, field), 'row')  58.8 us
    psum x1, blocking collectives, body(): curvature_now = lax.psum(per_component(direction, image), 'row')  26.8 us
    ppermute x4, starting transfers between devices, with_halo(): lax.ppermute(lax.slice_in_dim(block, block.shape[dim] - width, None, axis...  13.6 us
  transfers between devices with their start and end apart: 8, of which 3 were waited for; matrix products, arithmetic and copies ran while one was open for 38% of the time, Pallas kernels for 0%

commit v1 on v0

v1 whole, which is shorter than its diff:
```python
import functools
import math

import jax
import jax.numpy as jnp
from jax import lax
from jax.experimental import pallas as pl
from jax.experimental.pallas import tpu as pltpu
from jax.sharding import PartitionSpec as P

RADIUS = 0.9
DIAGONAL_SHIFT = 0.5
PHI_SCALE = 4.0 / RADIUS**5
CHUNK = 64
STEP = 32
VMEM_BYTES = 50 * 1024 * 1024
F32 = jnp.float32
BF16 = jnp.bfloat16


def vmem():
    return pl.BlockSpec(memory_space=pltpu.VMEM)


def anywhere():
    return pl.BlockSpec(memory_space=pl.ANY)


def greet(targets):
    barrier = pltpu.get_barrier_semaphore()
    for target in targets:
        pl.semaphore_signal(
            barrier, inc=1, device_id={"row": target}, device_id_type=pl.DeviceIdType.MESH
        )
    pl.semaphore_wait(barrier, len(targets))


def send(src, dst, send_sem, recv_sem, target):
    copy = pltpu.make_async_remote_copy(
        src_ref=src,
        dst_ref=dst,
        send_sem=send_sem,
        recv_sem=recv_sem,
        device_id={"row": target},
        device_id_type=pl.DeviceIdType.MESH,
    )
    copy.start()
    return copy


def halo_kernel(devices, total, *refs):
    sources, exts = refs[:total], refs[total : 2 * total]
    send_sems, recv_sems, own_sems = refs[2 * total :]
    me = lax.axis_index("row")
    right = lax.rem(me + 1, devices)
    left = lax.rem(me + devices - 1, devices)
    own = []
    for k in range(total):
        copy = pltpu.make_async_copy(sources[k], exts[k].at[1], own_sems.at[k])
        copy.start()
        own.append(copy)
    greet([left, right])
    copies = []
    for k in range(total):
        copies.append(
            send(sources[k], exts[k].at[0], send_sems.at[2 * k], recv_sems.at[2 * k], right)
        )
        copies.append(
            send(sources[k], exts[k].at[2], send_sems.at[2 * k + 1], recv_sems.at[2 * k + 1], left)
        )
    for copy in own:
        copy.wait()
    for copy in copies:
        copy.wait()


def with_halo(arrays, devices, collective_id):
    total = len(arrays)
    outs = pl.pallas_call(
        functools.partial(halo_kernel, devices, total),
        out_shape=[jax.ShapeDtypeStruct((3,) + a.shape, a.dtype) for a in arrays],
        in_specs=[anywhere()] * total,
        out_specs=[anywhere()] * total,
        scratch_shapes=[
            pltpu.SemaphoreType.DMA((2 * total,)),
            pltpu.SemaphoreType.DMA((2 * total,)),
            pltpu.SemaphoreType.DMA((total,)),
        ],
        compiler_params=pltpu.CompilerParams(collective_id=collective_id, has_side_effects=True),
    )(*arrays)
    return outs


def stack_rows(ref, box, width):
    rows = lax.broadcasted_iota(jnp.int32, (8, width), 0)
    stacked = jnp.zeros((8, width), F32)
    for k in range(3):
        row = jnp.broadcast_to(ref[box, pl.ds(k, 1), :], (8, width))
        stacked = jnp.where(rows == k, row, stacked)
    return stacked


def pair_kernel(
    boxes, nearby, slots, width, scale, shift,
    ids, live, own_counts, near_counts,
    own_points, near_points, near_values, *rest,
):
    if shift:
        own_values, out, columns, loads, high, low, acc = rest
    else:
        out, columns, loads, high, low, acc = rest
    lanes = lax.broadcasted_iota(jnp.int32, (8, width), 1)

    def prepare(box, carry):
        columns[box, :, 0:8] = stack_rows(near_points, box, width).T
        value = jnp.where(lanes < near_counts[box], stack_rows(near_values, box, width), 0.0)
        top = value.astype(BF16).astype(F32)
        loads[box] = jnp.concatenate([top, value - top], axis=0).astype(BF16)
        return carry

    lax.fori_loop(0, nearby, prepare, 0)
    loads[nearby] = jnp.zeros((16, width), BF16)
    high[...] = jnp.zeros_like(high)
    low[...] = jnp.zeros_like(low)
    acc[...] = jnp.zeros_like(acc)

    def add_pair(box, near, slot):
        value = loads[near]
        total = jnp.dot(value, high[slot], preferred_element_type=F32)
        total = total + jnp.dot(value, low[slot], preferred_element_type=F32)
        acc[box] += total

    def one_box(box, carry):
        wide = own_counts[box] > width // 2

        def one_slot(s, state):
            last_box, last_near, slot = state
            near = ids[box * slots + s]
            chunks = (near_counts[near] + (CHUNK - 1)) // CHUNK

            def variant(rows, span):
                add_pair(last_box, last_near, 1 - slot)
                points = [own_points[box, pl.ds(k, 1), 0:span] for k in range(3)]
                for j in range(0, rows, STEP):
                    squared = None
                    block = columns[near, j : j + STEP, 0:8]
                    for k in range(3):
                        along = block[:, k : k + 1] - points[k]
                        squared = along * along if squared is None else squared + along * along
                    squared = jnp.maximum(squared, 1e-30)
                    distance = squared * lax.rsqrt(squared)
                    falling = jnp.maximum(RADIUS - distance, 0.0)
                    falling = falling * falling
                    phi = falling * falling * (distance + 0.25 * RADIUS)
                    top = phi.astype(BF16)
                    high[slot, j : j + STEP, 0:span] = top
                    low[slot, j : j + STEP, 0:span] = (phi - top.astype(F32)).astype(BF16)

            for count in range(1, width // CHUNK + 1):
                for span in (width // 2, width):
                    is_wide = span == width

                    @pl.when(jnp.logical_and(chunks == count, wide == is_wide))
                    def _(count=count, span=span):
                        variant(count * CHUNK, span)

            return box, near, 1 - slot

        return lax.fori_loop(0, live[box], one_slot, carry)

    last_box, last_near, slot = lax.fori_loop(
        0, boxes, one_box, (jnp.int32(0), jnp.int32(nearby), jnp.int32(0))
    )
    add_pair(last_box, last_near, 1 - slot)

    def finish(box, carry):
        total = (acc[box, 0:8, :] + acc[box, 8:16, :]) * scale
        total = jnp.where(lanes < own_counts[box], total, 0.0)[0:3]
        if shift:
            total = total + shift * own_values[box]
        out[box] = total
        return carry

    lax.fori_loop(0, boxes, finish, 0)


def pair_terms(ids, live, own_counts, near_counts, own_points, near_points, near_values, scale, shift, own_values=None):
    boxes, slots = ids.shape
    nearby = near_points.shape[0]
    width = own_points.shape[2]
    operands = [own_points, near_points, near_values] + ([own_values] if shift else [])
    smem = pl.BlockSpec(memory_space=pltpu.SMEM)
    work = boxes * slots * width * width
    return pl.pallas_call(
        functools.partial(pair_kernel, boxes, nearby, slots, width, scale, shift),
        out_shape=jax.ShapeDtypeStruct((boxes, 3, width), F32),
        in_specs=[smem] * 4 + [vmem()] * len(operands),
        out_specs=vmem(),
        scratch_shapes=[
            pltpu.VMEM((nearby, width, 128), F32),
            pltpu.VMEM((nearby + 1, 16, width), BF16),
            pltpu.VMEM((2, width, width), BF16),
            pltpu.VMEM((2, width, width), BF16),
            pltpu.VMEM((boxes, 16, width), F32),
        ],
        compiler_params=pltpu.CompilerParams(vmem_limit_bytes=VMEM_BYTES),
        cost_estimate=pl.CostEstimate(flops=20 * work, bytes_accessed=1 << 20, transcendentals=work),
    )(ids.reshape(-1), live, own_counts, near_counts, *operands)


def lane_parts(first, second):
    total = jnp.sum(first * second, axis=0)
    half = total.shape[1] // 2
    return total[:, :half] + total[:, half:]


def gather_sums(devices, gathered, send_sems, recv_sems, me, base):
    copies = []
    for step in range(1, devices):
        target = lax.rem(me + step, devices)
        copies.append(
            send(
                gathered.at[me],
                gathered.at[me],
                send_sems.at[base + step],
                recv_sems.at[base + step],
                target,
            )
        )
    return copies


def whole_sum(gathered, first):
    rows = jnp.sum(gathered[:, first : first + 3, :], axis=0)
    return jnp.sum(rows, axis=1, keepdims=True)


def first_kernel(devices, rhs, image, direction, coefs, landed, gathered, send_sems, recv_sems):
    me = lax.axis_index("row")
    right = lax.rem(me + 1, devices)
    left = lax.rem(me + devices - 1, devices)
    base = rhs[1]
    mine = image[...]
    gathered[me] = jnp.zeros(gathered.shape[1:], F32)
    gathered[me, 0:3] = lane_parts(base, base)
    gathered[me, 3:6] = lane_parts(base, mine)
    gathered[me, 6:9] = lane_parts(mine, mine)
    greet([lax.rem(me + step, devices) for step in range(1, devices)])
    copies = gather_sums(devices, gathered, send_sems, recv_sems, me, 1)
    copies.append(send(image, landed.at[0], send_sems.at[0], recv_sems.at[0], right))
    copies.append(send(image, landed.at[1], send_sems.at[1], recv_sems.at[1], left))
    for copy in copies:
        copy.wait()
    norm = whole_sum(gathered, 0)
    alpha = norm / whole_sum(gathered, 3)
    norm_next = norm - 2.0 * alpha * whole_sum(gathered, 3) + alpha * alpha * whole_sum(gathered, 6)
    beta = norm_next / norm
    coefs[...] = jnp.zeros_like(coefs)
    coefs[0:3] = jnp.broadcast_to(alpha, (3, coefs.shape[1]))
    coefs[3:6] = jnp.broadcast_to(norm_next, (3, coefs.shape[1]))
    direction[0] = (rhs[0] - alpha[None] * landed[0]) + beta[None] * rhs[0]
    direction[1] = (base - alpha[None] * mine) + beta[None] * base
    direction[2] = (rhs[2] - alpha[None] * landed[1]) + beta[None] * rhs[2]


def last_kernel(devices, rhs, image, direction, second, coefs, mapped, residual, gathered, send_sems, recv_sems):
    me = lax.axis_index("row")
    base = rhs[1]
    along = direction[1]
    gathered[me] = jnp.zeros(gathered.shape[1:], F32)
    gathered[me, 0:3] = lane_parts(along, second[...])
    greet([lax.rem(me + step, devices) for step in range(1, devices)])
    for copy in gather_sums(devices, gathered, send_sems, recv_sems, me, -1):
        copy.wait()
    alpha = coefs[0:3, 0:1][None]
    alpha_next = (coefs[3:6, 0:1] / whole_sum(gathered, 0))[None]
    mapped[...] = alpha * base + alpha_next * along
    residual[...] = (base - alpha * image[...]) - alpha_next * second[...]


def body(solid_points, solid_counts, fluid_points, fluid_forces, fluid_counts, ss_pairs, sf_pairs):
    boxes, _, width = solid_points.shape
    fluids = fluid_points.shape[0]
    devices = lax.axis_size("row")
    me = lax.axis_index("row")
    count_lanes = -(-max(boxes, fluids) // 128) * 128
    counts = jnp.zeros((8, count_lanes), jnp.int32)
    counts = counts.at[0, :fluids].set(fluid_counts).at[1, :boxes].set(solid_counts)
    near_solid, near_fluid, near_forces, near_counts = with_halo(
        [solid_points, fluid_points, fluid_forces, counts], devices, 0
    )
    near_fluid = near_fluid.reshape(3 * fluids, 3, width)
    near_forces = near_forces.reshape(3 * fluids, 3, width)
    near_solid = near_solid.reshape(3 * boxes, 3, width)
    near_fluid_counts = near_counts[:, 0, :fluids].reshape(-1)
    near_solid_counts = near_counts[:, 1, :boxes].reshape(-1)
    sf_live = jnp.sum((sf_pairs >= 0).astype(jnp.int32), axis=1)
    ss_live = jnp.sum((ss_pairs >= 0).astype(jnp.int32), axis=1)
    sf_ids = jnp.clip(sf_pairs - (me - 1) * fluids, 0, 3 * fluids - 1)
    ss_ids = jnp.clip(ss_pairs - (me - 1) * boxes, 0, 3 * boxes - 1)

    rhs = pair_terms(
        sf_ids, sf_live, solid_counts, near_fluid_counts,
        solid_points, near_fluid, near_forces,
        PHI_SCALE / math.sqrt(width), 0.0,
    )
    (near_rhs,) = with_halo([rhs], devices, 1)

    def operate(near, own):
        return pair_terms(
            ss_ids, ss_live, solid_counts, near_solid_counts,
            solid_points, near_solid, near.reshape(3 * boxes, 3, width),
            PHI_SCALE / width, DIAGONAL_SHIFT, own,
        )

    image = operate(near_rhs, rhs)
    block = jax.ShapeDtypeStruct((boxes, 3, width), F32)
    direction, coefs = pl.pallas_call(
        functools.partial(first_kernel, devices),
        out_shape=[
            jax.ShapeDtypeStruct((3, boxes, 3, width), F32),
            jax.ShapeDtypeStruct((8, 128), F32),
        ],
        in_specs=[vmem()] * 2,
        out_specs=[vmem()] * 2,
        scratch_shapes=[
            pltpu.VMEM((2, boxes, 3, width), F32),
            pltpu.VMEM((devices, 16, width // 2), F32),
            pltpu.SemaphoreType.DMA((devices + 1,)),
            pltpu.SemaphoreType.DMA((devices + 1,)),
        ],
        compiler_params=pltpu.CompilerParams(collective_id=2, has_side_effects=True),
    )(near_rhs, image)
    second = operate(direction, direction[1])
    return tuple(
        pl.pallas_call(
            functools.partial(last_kernel, devices),
            out_shape=[block, block],
            in_specs=[vmem()] * 5,
            out_specs=[vmem()] * 2,
            scratch_shapes=[
                pltpu.VMEM((devices, 16, width // 2), F32),
                pltpu.SemaphoreType.DMA((devices - 1,)),
                pltpu.SemaphoreType.DMA((devices - 1,)),
            ],
            compiler_params=pltpu.CompilerParams(collective_id=3, has_side_effects=True),
        )(near_rhs, image, direction, second, coefs)
    )


def solution(mesh):
    return jax.shard_map(
        body,
        mesh=mesh,
        in_specs=(
            P(("parts", "row"), None, None),
            P(("parts", "row")),
            P(("parts", "row"), None, None),
            P(("parts", "row"), None, None),
            P(("parts", "row")),
            P(("parts", "row"), None),
            P(("parts", "row"), None),
        ),
        out_specs=(P(("parts", "row"), None, None), P(("parts", "row"), None, None)),
        check_vma=False,
    )
```

time: 513 us -> 302 us (0.59)
  matrix products: 362 us -> 0 us
  Pallas kernels: 0 us -> 281 us
  blocking collectives: 85.6 us -> 0 us
  starting transfers between devices: 22 us -> 0 us
  waiting for transfers between devices: 8.78 us -> 0 us
  other arithmetic: 6.87 us -> 0.13 us
    dot_general x12 -> x0, matrix products: 362 us -> none  [add_group(): jnp.einsum('sgij,sgcj->sci', kernel, carried, precision=lax.Precision.HIG...]
    pallas_call x0 -> x7, Pallas kernels: none -> 281 us  [the longest x3 241 us: pair_terms(): pl.pallas_call(functools.partial(pair_kernel, boxes, nearby, slots, width...]
    psum x3 -> x0, blocking collectives: 85.6 us -> none  [the longest x2 58.8 us: squared_norm(): return lax.psum(per_component(field, field), 'row')]
    ppermute x8 -> x0, starting transfers between devices: 22 us -> none  [the longest x4 13.6 us: with_halo(): lax.ppermute(lax.slice_in_dim(block, block.shape[dim] - width, None, axis...]
    gather x24 -> x0, local copies, waits for them, and re-layouts: 17.7 us -> none  [the longest x12 8.83 us: add_group(): jnp.take(values, position, axis=0)]
    unnamed x17 -> x39, local copies, waits for them, and re-layouts: 1.47 us -> 12 us
    ppermute x8 -> x0, waiting for transfers between devices: 8.78 us -> none  [the longest x4 6.75 us: with_halo(): lax.ppermute(lax.slice_in_dim(block, 0, width, axis=dim), axis, backward)]
  transfers between devices with their start and end apart: 8 -> 0, of which waited for: 3 -> 0; matrix products, arithmetic and copies ran while one was open for 38% -> 0% of each run, Pallas kernels for 0% -> 0%
where the time goes in v1:
time: 302 us; the launch traced here: 299 us
  Pallas kernels  281 us (93%)
  local copies, waits for them, and re-layouts  17.1 us (6%)
    pallas_call x3, Pallas kernels, pair_terms(): pl.pallas_call(functools.partial(pair_kernel, boxes, nearby, slots, width...  241 us
    pallas_call x2, Pallas kernels, with_halo(): pl.pallas_call(functools.partial(halo_kernel, devices, total), out_shape=...  23.5 us
    unnamed x39, local copies, waits for them, and re-layouts  12 us
    pallas_call x1, Pallas kernels, body(): pl.pallas_call(functools.partial(last_kernel, devices), out_shape=[block,...  8.53 us
    pallas_call x1, Pallas kernels, body(): pl.pallas_call(functools.partial(first_kernel, devices), out_shape=[jax.S...  8.48 us

profile of v1, /device:TPU:3, one launch (start us, length us, event | category | flops | bytes accessed | tf_op | source)
XLA Modules:
  0.0 299.3 jit_solution(10831976700166576054)
XLA Ops:
  0.6 1.6 copy.17.refs_0_.own_points
  2.2 0.8 copy.18.refs_1_
  3.1 0.8 copy.19.refs_2_
  3.9 0.7 copy-done.17
  4.6 0.7 copy-done.7
  5.9 16.3 %shard_map.86 = (f32[3,24,3,256]{3,2,1,0:T(4,128)}, f32[3,48,3,256]{3,2,1,0:T(4,128)}, f32[3,48,3,256]{3,2,1,0:T(4,128)}, s32[3,8,128]{2,1,0:T(8,128)}) custom-call(f32[24,3,256]{2,1,0:T(4,128)} %copy.17.refs_0_.own_points, f32[48,3,256]{2,1,0:T(4,128)} %copy.18.refs_1_, f32[48,3,256]{2,1,0:T(4,128)} %copy.19.refs_2_, s32[8,128]{1,0:T(8,128)} %copy-done.14), custom_call_target="tpu_custom_call" | custom-call | tf_op jit(solution)/shard_map/pallas_call | solution.py:79
  22.3 0.7 slice_reduce_fusion.1
  23.3 1.1 copy-done.8
  24.4 1.1 copy-done.9
  25.4 108.2 %shard_map.87.refs_0_.rest_0_ = f32[24,3,256]{2,1,0:T(4,128)S(1)} custom-call(s32[432]{0:T(512)S(1)} %reshape.85.ids, s32[24]{0:T(128)S(1)} %get-tuple-element.42.live, s32[24]{0:T(128)S(1)} %copy-done.7, s32[144]{0:T(256)S(1)} %reshape_squeeze.6.near_counts, f32[24,3,256]{2,1,0:T(4,128)S(1)} %copy-done.3, f32[144,3,256]{2,1,0:T(4,128)S(1)} %bitcast.12, ...), custom_call_target="tpu_custom_call" | custom-call | flops 566231040 | bytes 1048576 | tf_op jit(solution)/shard_map/pallas_call | solution.py:194
  133.7 0.6 copy-done.5
  134.3 7.2 %shard_map.88.rhs = f32[3,24,3,256]{3,2,1,0:T(4,128)} custom-call(f32[24,3,256]{2,1,0:T(4,128)} %copy-done.5), custom_call_target="tpu_custom_call" | custom-call | tf_op jit(solution)/shard_map/pallas_call | solution.py:79
  141.5 0.7 slice_reduce_fusion
  142.6 1.0 copy-done
  143.5 0.9 copy-done.6
  144.4 66.2 %shard_map.89.image = f32[24,3,256]{2,1,0:T(4,128)S(1)} custom-call(s32[216]{0:T(256)S(1)} %reshape.90.ids, s32[24]{0:T(128)S(1)} %get-tuple-element.44.live, s32[24]{0:T(128)S(1)} %copy-done.7, s32[72]{0:T(128)S(1)} %reshape_squeeze.7.near_counts, f32[24,3,256]{2,1,0:T(4,128)S(1)} %copy-done.3, f32[72,3,256]{2,1,0:T(4,128)S(1)} %bitcast.14, ...), custom_call_target="tpu_custom_call" | custom-call | flops 283115520 | bytes 1048576 | tf_op jit(solution)/shard_map/pallas_call | solution.py:194
  210.6 0.6 copy-done.2
  211.3 8.5 %shard_map.90 = (f32[3,24,3,256]{3,2,1,0:T(4,128)}, f32[8,128]{1,0:T(8,128)}) custom-call(f32[3,24,3,256]{3,2,1,0:T(4,128)} %shard_map.88.rhs, f32[24,3,256]{2,1,0:T(4,128)} %copy-done.2), custom_call_target="tpu_custom_call" | custom-call | tf_op jit(solution)/shard_map/pallas_call | solution.py:318
  219.8 0.9 slice_bitcast_fusion.rest_0_
  220.7 1.0 copy-done.1
  221.6 66.2 %shard_map.91.second = f32[24,3,256]{2,1,0:T(4,128)S(1)} custom-call(s32[216]{0:T(256)S(1)} %reshape.90.ids, s32[24]{0:T(128)S(1)} %get-tuple-element.44.live, s32[24]{0:T(128)S(1)} %copy-done.7, s32[72]{0:T(128)S(1)} %reshape_squeeze.7.near_counts, f32[24,3,256]{2,1,0:T(4,128)S(1)} %copy-done.3, f32[72,3,256]{2,1,0:T(4,128)S(1)} %bitcast.15, ...), custom_call_target="tpu_custom_call" | custom-call | flops 283115520 | bytes 1048576 | tf_op jit(solution)/shard_map/pallas_call | solution.py:194
  288.5 8.5 %shard_map.92 = (f32[24,3,256]{2,1,0:T(4,128)}, f32[24,3,256]{2,1,0:T(4,128)}) custom-call(f32[3,24,3,256]{3,2,1,0:T(4,128)} %shard_map.88.rhs, f32[24,3,256]{2,1,0:T(4,128)} %copy-done.2, f32[3,24,3,256]{3,2,1,0:T(4,128)} %get-tuple-element.36.direction, f32[24,3,256]{2,1,0:T(4,128)} %copy-done.4, f32[8,128]{1,0:T(8,128)} %get-tuple-element.37.coefs), custom_call_target="tpu_custom_call" | custom-call | tf_op jit(solution)/shard_map/pallas_call | solution.py:336
  297.0 1.6 copy.24
  298.6 0.6 copy.25
  (36 shorter events, 2.1 us)
Async XLA Ops:
  0.6 1.6 copy-start.11
  2.2 0.9 copy-start.12
  3.9 0.7 copy-start.17
  4.6 0.7 copy-start.7
  5.3 0.6 copy-start.14
  5.9 17.4 %copy-start.3 = (f32[24,3,256]{2,1,0:T(4,128)S(1)}, f32[24,3,256]{2,1,0:T(4,128)}, u32[]{:S(2)}) copy-start(f32[24,3,256]{2,1,0:T(4,128)} %copy.17.refs_0_.own_points) | copy-start | bytes 221188
  22.3 0.8 copy-start.15
  23.3 1.1 copy-start.8
  24.4 1.1 copy-start.9
  133.7 0.6 copy-start.5
  134.3 8.2 %copy-start.10 = (f32[3,24,3,256]{3,2,1,0:T(4,128)S(1)}, f32[3,24,3,256]{3,2,1,0:T(4,128)}, u32[]{:S(2)}) copy-start(f32[3,24,3,256]{3,2,1,0:T(4,128)} %get-tuple-element.35) | copy-start | bytes 663556
  141.5 0.8 copy-start.16
  142.5 1.0 copy-start
  143.5 0.9 copy-start.6
  210.6 0.6 copy-start.2
  220.7 1.0 copy-start.1
  287.9 0.6 copy-start.4
  297.0 1.6 copy-start.13

commit v2 on v1

--- a/solution.py
+++ b/solution.py
@@ -11,9 +11,11 @@
 RADIUS = 0.9
 DIAGONAL_SHIFT = 0.5
 PHI_SCALE = 4.0 / RADIUS**5
-CHUNK = 64
+CHUNK = 32
+GROUP = 4
+LANES = 128
 STEP = 32
-VMEM_BYTES = 50 * 1024 * 1024
+VMEM_BYTES = 32 * 1024 * 1024
 F32 = jnp.float32
 BF16 = jnp.bfloat16
 
@@ -102,7 +104,7 @@
 
 def pair_kernel(
     boxes, nearby, slots, width, scale, shift,
-    ids, live, own_counts, near_counts,
+    load_ids, point_ids, groups, own_counts, near_counts,
     own_points, near_points, near_values, *rest,
 ):
     if shift:
@@ -112,40 +114,55 @@
     lanes = lax.broadcasted_iota(jnp.int32, (8, width), 1)
 
     def prepare(box, carry):
-        columns[box, :, 0:8] = stack_rows(near_points, box, width).T
         value = jnp.where(lanes < near_counts[box], stack_rows(near_values, box, width), 0.0)
         top = value.astype(BF16).astype(F32)
-        loads[box] = jnp.concatenate([top, value - top], axis=0).astype(BF16)
+        middle = (value - top).astype(BF16).astype(F32)
+        terms = [top, middle, value - top - middle, jnp.zeros_like(value)]
+        terms = jnp.concatenate(terms, axis=0).astype(BF16)
+        loads[2 * box + 1] = terms[:, :LANES]
+        loads[2 * box + 2] = terms[:, LANES:]
         return carry
 
-    lax.fori_loop(0, nearby, prepare, 0)
-    loads[nearby] = jnp.zeros((16, width), BF16)
+    lax.fori_loop(0, nearby, prepare, 0, unroll=8)
+    loads[0] = jnp.zeros(loads.shape[1:], BF16)
     high[...] = jnp.zeros_like(high)
     low[...] = jnp.zeros_like(low)
-    acc[...] = jnp.zeros_like(acc)
-
-    def add_pair(box, near, slot):
-        value = loads[near]
-        total = jnp.dot(value, high[slot], preferred_element_type=F32)
-        total = total + jnp.dot(value, low[slot], preferred_element_type=F32)
-        acc[box] += total
-
-    def one_box(box, carry):
-        wide = own_counts[box] > width // 2
-
-        def one_slot(s, state):
-            last_box, last_near, slot = state
-            near = ids[box * slots + s]
-            chunks = (near_counts[near] + (CHUNK - 1)) // CHUNK
-
-            def variant(rows, span):
-                add_pair(last_box, last_near, 1 - slot)
-                points = [own_points[box, pl.ds(k, 1), 0:span] for k in range(3)]
-                for j in range(0, rows, STEP):
+
+    def box_rows(box, rows):
+        turned = stack_rows(own_points, box, width).T[0:rows]
+        for k in range(3):
+            columns[k, 0:rows, :] = jnp.broadcast_to(turned[:, k : k + 1], (rows, LANES))
+        acc[...] = jnp.zeros_like(acc)
+
+        def add_group(units, slot):
+            value = jnp.concatenate([loads[unit] for unit in units], axis=1)
+            total = None
+            for part in (high, low):
+                term = lax.dot_general(
+                    value, part[slot, 0:rows, :], (((1,), (1,)), ((), ())),
+                    preferred_element_type=F32,
+                )
+                total = term if total is None else total + term
+            acc[:, 0:rows] += total
+
+        def one_group(g, state):
+            slot = state[0]
+            add_group(state[1:], 1 - slot)
+            first = box * slots + g * GROUP
+            points = []
+            for unit in range(GROUP):
+                place = point_ids[first + unit]
+                near = place // 2
+                lane = pl.multiple_of((place % 2) * LANES, LANES)
+                points.append(
+                    [near_points[near, pl.ds(k, 1), pl.ds(lane, LANES)] for k in range(3)]
+                )
+            for j in range(0, rows, STEP):
+                own = [columns[k, j : j + STEP, :] for k in range(3)]
+                for unit in range(GROUP):
                     squared = None
-                    block = columns[near, j : j + STEP, 0:8]
                     for k in range(3):
-                        along = block[:, k : k + 1] - points[k]
+                        along = own[k] - points[unit][k]
                         squared = along * along if squared is None else squared + along * along
                     squared = jnp.maximum(squared, 1e-30)
                     distance = squared * lax.rsqrt(squared)
@@ -153,35 +170,50 @@
                     falling = falling * falling
                     phi = falling * falling * (distance + 0.25 * RADIUS)
                     top = phi.astype(BF16)
-                    high[slot, j : j + STEP, 0:span] = top
-                    low[slot, j : j + STEP, 0:span] = (phi - top.astype(F32)).astype(BF16)
-
-            for count in range(1, width // CHUNK + 1):
-                for span in (width // 2, width):
-                    is_wide = span == width
-
-                    @pl.when(jnp.logical_and(chunks == count, wide == is_wide))
-                    def _(count=count, span=span):
-                        variant(count * CHUNK, span)
-
-            return box, near, 1 - slot
-
-        return lax.fori_loop(0, live[box], one_slot, carry)
-
-    last_box, last_near, slot = lax.fori_loop(
-        0, boxes, one_box, (jnp.int32(0), jnp.int32(nearby), jnp.int32(0))
-    )
-    add_pair(last_box, last_near, 1 - slot)
-
-    def finish(box, carry):
-        total = (acc[box, 0:8, :] + acc[box, 8:16, :]) * scale
+                    where = pl.ds(unit * LANES, LANES)
+                    high[slot, j : j + STEP, where] = top
+                    low[slot, j : j + STEP, where] = (phi - top.astype(F32)).astype(BF16)
+            return (1 - slot,) + tuple(load_ids[first + unit] for unit in range(GROUP))
+
+        zero = jnp.int32(0)
+        state = lax.fori_loop(0, groups[box], one_group, (zero,) * (GROUP + 1))
+        add_group(state[1:], 1 - state[0])
+        total = (acc[0:8] + (acc[8:16] + acc[16:24])) * scale
         total = jnp.where(lanes < own_counts[box], total, 0.0)[0:3]
         if shift:
             total = total + shift * own_values[box]
         out[box] = total
+
+    def one_box(box, carry):
+        chunks = jnp.maximum((own_counts[box] + (CHUNK - 1)) // CHUNK, 2)
+        for count in range(2, width // CHUNK + 1):
+
+            @pl.when(chunks == count)
+            def _(count=count):
+                box_rows(box, count * CHUNK)
+
         return carry
 
-    lax.fori_loop(0, boxes, finish, 0)
+    lax.fori_loop(0, boxes, one_box, 0)
+
+
+def unit_lists(ids, live, near_counts):
+    boxes, slots = ids.shape
+    nearby = near_counts.shape[0]
+    chosen = ids[:, :, None] == jnp.arange(nearby, dtype=jnp.int32)
+    counts = jnp.sum(jnp.where(chosen, near_counts, 0), axis=2)
+    used = jnp.arange(slots, dtype=jnp.int32)[None] < live[:, None]
+    flags = jnp.stack([used, used & (counts > LANES)], axis=2).reshape(boxes, 2 * slots)
+    units = jnp.stack([2 * ids + 1, 2 * ids + 2], axis=2).reshape(boxes, 2 * slots)
+    entry = jnp.arange(2 * slots, dtype=jnp.int32)
+    before = flags[:, None, :] & (entry[None, :] < entry[:, None])[None]
+    place = jnp.where(flags, jnp.sum(before.astype(jnp.int32), axis=2), -1)
+    length = -(-2 * slots // GROUP) * GROUP
+    target = place[:, None, :] == jnp.arange(length, dtype=jnp.int32)[None, :, None]
+    load_ids = jnp.sum(jnp.where(target, units[:, None, :], 0), axis=2)
+    point_ids = jnp.where(load_ids > 0, load_ids, load_ids[:, :1]) - 1
+    total = jnp.sum(flags.astype(jnp.int32), axis=1)
+    return load_ids, point_ids, (total + (GROUP - 1)) // GROUP
 
 
 def pair_terms(ids, live, own_counts, near_counts, own_points, near_points, near_values, scale, shift, own_values=None):
@@ -191,21 +223,24 @@
     operands = [own_points, near_points, near_values] + ([own_values] if shift else [])
     smem = pl.BlockSpec(memory_space=pltpu.SMEM)
     work = boxes * slots * width * width
+    load_ids, point_ids, groups = unit_lists(ids, live, near_counts)
     return pl.pallas_call(
-        functools.partial(pair_kernel, boxes, nearby, slots, width, scale, shift),
+        functools.partial(
+            pair_kernel, boxes, nearby, load_ids.shape[1], width, scale, shift
+        ),
         out_shape=jax.ShapeDtypeStruct((boxes, 3, width), F32),
-        in_specs=[smem] * 4 + [vmem()] * len(operands),
+        in_specs=[smem] * 5 + [vmem()] * len(operands),
         out_specs=vmem(),
         scratch_shapes=[
-            pltpu.VMEM((nearby, width, 128), F32),
-            pltpu.VMEM((nearby + 1, 16, width), BF16),
-            pltpu.VMEM((2, width, width), BF16),
-            pltpu.VMEM((2, width, width), BF16),
-            pltpu.VMEM((boxes, 16, width), F32),
+            pltpu.VMEM((3, width, LANES), F32),
+            pltpu.VMEM((2 * nearby + 1, 32, LANES), BF16),
+            pltpu.VMEM((2, width, GROUP * LANES), BF16),
+            pltpu.VMEM((2, width, GROUP * LANES), BF16),
+            pltpu.VMEM((32, width), F32),
         ],
         compiler_params=pltpu.CompilerParams(vmem_limit_bytes=VMEM_BYTES),
         cost_estimate=pl.CostEstimate(flops=20 * work, bytes_accessed=1 << 20, transcendentals=work),
-    )(ids.reshape(-1), live, own_counts, near_counts, *operands)
+    )(load_ids.reshape(-1), point_ids.reshape(-1), groups, own_counts, near_counts, *operands)
 
 
 def lane_parts(first, second):

time: 302 us -> 225 us (0.75)
  Pallas kernels: 281 us -> 201 us
    pallas_call x3, Pallas kernels: 241 us -> 161 us  [pair_terms(): pl.pallas_call(functools.partial(pair_kernel, boxes, nearby, load_ids.sha...]
where the time goes in v2:
time: 225 us; the launch traced here: 222 us
  Pallas kernels  201 us (89%)
  local copies, waits for them, and re-layouts  17.4 us (8%)
  other arithmetic  3.06 us (1%)
    pallas_call x3, Pallas kernels, pair_terms(): pl.pallas_call(functools.partial(pair_kernel, boxes, nearby, load_ids.sha...  161 us
    pallas_call x2, Pallas kernels, with_halo(): pl.pallas_call(functools.partial(halo_kernel, devices, total), out_shape=...  22.8 us
    unnamed x39, local copies, waits for them, and re-layouts  11 us
    pallas_call x1, Pallas kernels, body(): pl.pallas_call(functools.partial(last_kernel, devices), out_shape=[block,...  8.54 us
    pallas_call x1, Pallas kernels, body(): pl.pallas_call(functools.partial(first_kernel, devices), out_shape=[jax.S...  8.47 us

profile of v2, /device:TPU:3, one launch (start us, length us, event | category | flops | bytes accessed | tf_op | source)
XLA Modules:
  0.0 222.5 jit_solution(10415291114961961092)
XLA Ops:
  0.6 1.6 copy.40.refs_0_.own_points
  2.2 0.8 copy.41.refs_1_
  3.1 0.8 copy.42.refs_2_
  3.9 0.7 copy-done.17
  4.6 0.7 copy-done.7
  5.9 16.3 %shard_map.86 = (f32[3,24,3,256]{3,2,1,0:T(4,128)}, f32[3,48,3,256]{3,2,1,0:T(4,128)}, f32[3,48,3,256]{3,2,1,0:T(4,128)}, s32[3,8,128]{2,1,0:T(8,128)}) custom-call(f32[24,3,256]{2,1,0:T(4,128)} %copy.40.refs_0_.own_points, f32[48,3,256]{2,1,0:T(4,128)} %copy.41.refs_1_, f32[48,3,256]{2,1,0:T(4,128)} %copy.42.refs_2_, s32[8,128]{1,0:T(8,128)} %copy-done.14), custom_call_target="tpu_custom_call" | custom-call | tf_op jit(solution)/shard_map/pallas_call | solution.py:81
  22.3 0.8 slice_reduce_fusion
  24.6 0.7 slice_reduce_fusion.1
  26.6 0.7 convert_reduce_fusion
  27.6 0.7 select_reduce_fusion
  28.7 1.1 copy-done.9
  29.8 65.8 %shard_map.87.refs_0_.rest_0_ = f32[24,3,256]{2,1,0:T(4,128)S(1)} custom-call(s32[864]{0:T(1024)S(1)} %reshape.278.load_ids, s32[864]{0:T(1024)S(1)} %fusion.point_ids, s32[24]{0:T(128)S(1)} %and_select_fusion.1.groups, s32[24]{0:T(128)S(1)} %copy-done.7, s32[144]{0:T(256)S(1)} %reshape_squeeze.6.near_counts, f32[24,3,256]{2,1,0:T(4,128)S(1)} %copy-done.3, ...), custom_call_target="tpu_custom_call" | custom-call | flops 566231040 | bytes 1048576 | tf_op jit(solution)/shard_map/pallas_call | solution.py:227
  95.6 0.6 copy-done.5
  96.2 6.5 %shard_map.88.rhs = f32[3,24,3,256]{3,2,1,0:T(4,128)} custom-call(f32[24,3,256]{2,1,0:T(4,128)} %copy-done.5), custom_call_target="tpu_custom_call" | custom-call | tf_op jit(solution)/shard_map/pallas_call | solution.py:81
  102.7 1.0 copy-done
  103.7 0.9 copy-done.6
  104.6 47.6 %shard_map.89.image = f32[24,3,256]{2,1,0:T(4,128)S(1)} custom-call(s32[480]{0:T(512)S(1)} %reshape.282.load_ids, s32[480]{0:T(512)S(1)} %fusion.1.point_ids, s32[24]{0:T(128)S(1)} %and_select_fusion.groups, s32[24]{0:T(128)S(1)} %copy-done.7, s32[72]{0:T(128)S(1)} %reshape_squeeze.7.near_counts, f32[24,3,256]{2,1,0:T(4,128)S(1)} %copy-done.3, ...), custom_call_target="tpu_custom_call" | custom-call | flops 283115520 | bytes 1048576 | tf_op jit(solution)/shard_map/pallas_call | solution.py:227
  152.9 8.5 %shard_map.90 = (f32[3,24,3,256]{3,2,1,0:T(4,128)}, f32[8,128]{1,0:T(8,128)}) custom-call(f32[3,24,3,256]{3,2,1,0:T(4,128)} %shard_map.88.rhs, f32[24,3,256]{2,1,0:T(4,128)} %copy-done.2), custom_call_target="tpu_custom_call" | custom-call | tf_op jit(solution)/shard_map/pallas_call | solution.py:353
  161.3 0.9 slice_bitcast_fusion.rest_0_
  162.3 1.0 copy-done.1
  163.2 47.8 %shard_map.91.second = f32[24,3,256]{2,1,0:T(4,128)S(1)} custom-call(s32[480]{0:T(512)S(1)} %reshape.282.load_ids, s32[480]{0:T(512)S(1)} %fusion.1.point_ids, s32[24]{0:T(128)S(1)} %and_select_fusion.groups, s32[24]{0:T(128)S(1)} %copy-done.7, s32[72]{0:T(128)S(1)} %reshape_squeeze.7.near_counts, f32[24,3,256]{2,1,0:T(4,128)S(1)} %copy-done.3, ...), custom_call_target="tpu_custom_call" | custom-call | flops 283115520 | bytes 1048576 | tf_op jit(solution)/shard_map/pallas_call | solution.py:227
  211.7 8.5 %shard_map.92 = (f32[24,3,256]{2,1,0:T(4,128)}, f32[24,3,256]{2,1,0:T(4,128)}) custom-call(f32[3,24,3,256]{3,2,1,0:T(4,128)} %shard_map.88.rhs, f32[24,3,256]{2,1,0:T(4,128)} %copy-done.2, f32[3,24,3,256]{3,2,1,0:T(4,128)} %get-tuple-element.36.direction, f32[24,3,256]{2,1,0:T(4,128)} %copy-done.4, f32[8,128]{1,0:T(8,128)} %get-tuple-element.37.coefs), custom_call_target="tpu_custom_call" | custom-call | tf_op jit(solution)/shard_map/pallas_call | solution.py:371
  220.2 1.6 copy.57
  221.8 0.6 copy.58
  (80 shorter events, 5.5 us)
Async XLA Ops:
  0.6 1.6 copy-start.11
  2.2 0.9 copy-start.12
  3.9 0.7 copy-start.17
  4.6 0.7 copy-start.7
  5.3 0.6 copy-start.14
  5.9 17.2 %copy-start.16 = (s32[24,9]{0,1:T(8,128)S(1)}, s32[24,9]{0,1:T(8,128)}, u32[]{:S(2)}) copy-start(s32[24,9]{0,1:T(8,128)} %param.16) | copy-start | bytes 2596
  5.9 19.4 %copy-start.15 = (s32[24,18]{1,0:T(8,128)S(1)}, s32[24,18]{1,0:T(8,128)}, u32[]{:S(2)}) copy-start(s32[24,18]{1,0:T(8,128)} %param.17) | copy-start | bytes 5188
  22.3 6.4 %copy-start.8 = (f32[3,48,3,256]{3,2,1,0:T(4,128)S(1)}, f32[3,48,3,256]{3,2,1,0:T(4,128)}, u32[]{:S(2)}) copy-start(f32[3,48,3,256]{3,2,1,0:T(4,128)} %get-tuple-element.33) | copy-start | bytes 1327108
  27.5 1.2 copy-start.3
  28.7 1.1 copy-start.9
  95.6 0.6 copy-start.5
  96.2 6.5 %copy-start.10 = (f32[3,24,3,256]{3,2,1,0:T(4,128)S(1)}, f32[3,24,3,256]{3,2,1,0:T(4,128)}, u32[]{:S(2)}) copy-start(f32[3,24,3,256]{3,2,1,0:T(4,128)} %get-tuple-element.35) | copy-start | bytes 663556
  102.7 1.0 copy-start
  103.7 0.9 copy-start.6
  152.2 0.6 copy-start.2
  162.3 1.0 copy-start.1
  211.0 0.6 copy-start.4
  220.2 1.6 copy-start.13

commit v3 on v2

--- a/solution.py
+++ b/solution.py
@@ -12,7 +12,6 @@
 DIAGONAL_SHIFT = 0.5
 PHI_SCALE = 4.0 / RADIUS**5
 CHUNK = 32
-GROUP = 4
 LANES = 128
 STEP = 32
 VMEM_BYTES = 32 * 1024 * 1024
@@ -103,7 +102,7 @@
 
 
 def pair_kernel(
-    boxes, nearby, slots, width, scale, shift,
+    boxes, nearby, slots, group, width, scale, shift,
     load_ids, point_ids, groups, own_counts, near_counts,
     own_points, near_points, near_values, *rest,
 ):
@@ -148,9 +147,9 @@
         def one_group(g, state):
             slot = state[0]
             add_group(state[1:], 1 - slot)
-            first = box * slots + g * GROUP
+            first = box * slots + g * group
             points = []
-            for unit in range(GROUP):
+            for unit in range(group):
                 place = point_ids[first + unit]
                 near = place // 2
                 lane = pl.multiple_of((place % 2) * LANES, LANES)
@@ -159,7 +158,7 @@
                 )
             for j in range(0, rows, STEP):
                 own = [columns[k, j : j + STEP, :] for k in range(3)]
-                for unit in range(GROUP):
+                for unit in range(group):
                     squared = None
                     for k in range(3):
                         along = own[k] - points[unit][k]
@@ -173,10 +172,10 @@
                     where = pl.ds(unit * LANES, LANES)
                     high[slot, j : j + STEP, where] = top
                     low[slot, j : j + STEP, where] = (phi - top.astype(F32)).astype(BF16)
-            return (1 - slot,) + tuple(load_ids[first + unit] for unit in range(GROUP))
+            return (1 - slot,) + tuple(load_ids[first + unit] for unit in range(group))
 
         zero = jnp.int32(0)
-        state = lax.fori_loop(0, groups[box], one_group, (zero,) * (GROUP + 1))
+        state = lax.fori_loop(0, groups[box], one_group, (zero,) * (group + 1))
         add_group(state[1:], 1 - state[0])
         total = (acc[0:8] + (acc[8:16] + acc[16:24])) * scale
         total = jnp.where(lanes < own_counts[box], total, 0.0)[0:3]
@@ -197,7 +196,7 @@
     lax.fori_loop(0, boxes, one_box, 0)
 
 
-def unit_lists(ids, live, near_counts):
+def unit_lists(ids, live, near_counts, group):
     boxes, slots = ids.shape
     nearby = near_counts.shape[0]
     chosen = ids[:, :, None] == jnp.arange(nearby, dtype=jnp.int32)
@@ -208,25 +207,25 @@
     entry = jnp.arange(2 * slots, dtype=jnp.int32)
     before = flags[:, None, :] & (entry[None, :] < entry[:, None])[None]
     place = jnp.where(flags, jnp.sum(before.astype(jnp.int32), axis=2), -1)
-    length = -(-2 * slots // GROUP) * GROUP
+    length = -(-2 * slots // group) * group
     target = place[:, None, :] == jnp.arange(length, dtype=jnp.int32)[None, :, None]
     load_ids = jnp.sum(jnp.where(target, units[:, None, :], 0), axis=2)
     point_ids = jnp.where(load_ids > 0, load_ids, load_ids[:, :1]) - 1
     total = jnp.sum(flags.astype(jnp.int32), axis=1)
-    return load_ids, point_ids, (total + (GROUP - 1)) // GROUP
-
-
-def pair_terms(ids, live, own_counts, near_counts, own_points, near_points, near_values, scale, shift, own_values=None):
+    return load_ids, point_ids, (total + (group - 1)) // group
+
+
+def pair_terms(ids, live, own_counts, near_counts, own_points, near_points, near_values, group, scale, shift, own_values=None):
     boxes, slots = ids.shape
     nearby = near_points.shape[0]
     width = own_points.shape[2]
     operands = [own_points, near_points, near_values] + ([own_values] if shift else [])
     smem = pl.BlockSpec(memory_space=pltpu.SMEM)
     work = boxes * slots * width * width
-    load_ids, point_ids, groups = unit_lists(ids, live, near_counts)
+    load_ids, point_ids, groups = unit_lists(ids, live, near_counts, group)
     return pl.pallas_call(
         functools.partial(
-            pair_kernel, boxes, nearby, load_ids.shape[1], width, scale, shift
+            pair_kernel, boxes, nearby, load_ids.shape[1], group, width, scale, shift
         ),
         out_shape=jax.ShapeDtypeStruct((boxes, 3, width), F32),
         in_specs=[smem] * 5 + [vmem()] * len(operands),
@@ -234,8 +233,8 @@
         scratch_shapes=[
             pltpu.VMEM((3, width, LANES), F32),
             pltpu.VMEM((2 * nearby + 1, 32, LANES), BF16),
-            pltpu.VMEM((2, width, GROUP * LANES), BF16),
-            pltpu.VMEM((2, width, GROUP * LANES), BF16),
+            pltpu.VMEM((2, width, group * LANES), BF16),
+            pltpu.VMEM((2, width, group * LANES), BF16),
             pltpu.VMEM((32, width), F32),
         ],
         compiler_params=pltpu.CompilerParams(vmem_limit_bytes=VMEM_BYTES),
@@ -318,17 +317,28 @@
     fluids = fluid_points.shape[0]
     devices = lax.axis_size("row")
     me = lax.axis_index("row")
-    count_lanes = -(-max(boxes, fluids) // 128) * 128
-    counts = jnp.zeros((8, count_lanes), jnp.int32)
-    counts = counts.at[0, :fluids].set(fluid_counts).at[1, :boxes].set(solid_counts)
-    near_solid, near_fluid, near_forces, near_counts = with_halo(
-        [solid_points, fluid_points, fluid_forces, counts], devices, 0
-    )
-    near_fluid = near_fluid.reshape(3 * fluids, 3, width)
-    near_forces = near_forces.reshape(3 * fluids, 3, width)
-    near_solid = near_solid.reshape(3 * boxes, 3, width)
-    near_fluid_counts = near_counts[:, 0, :fluids].reshape(-1)
-    near_solid_counts = near_counts[:, 1, :boxes].reshape(-1)
+    def count_rows(counts):
+        rows = -(-counts.shape[0] // (8 * LANES)) * 8
+        padded = jnp.zeros((rows * LANES,), F32).at[: counts.shape[0]].set(counts.astype(F32))
+        return padded.reshape(rows, LANES)
+
+    parts = [
+        solid_points.reshape(-1, LANES),
+        fluid_points.reshape(-1, LANES),
+        fluid_forces.reshape(-1, LANES),
+        count_rows(solid_counts),
+        count_rows(fluid_counts),
+    ]
+    (landed,) = with_halo([jnp.concatenate(parts, axis=0)], devices, 0)
+    pieces, first = [], 0
+    for part in parts:
+        pieces.append(landed[:, first : first + part.shape[0]])
+        first += part.shape[0]
+    near_solid = pieces[0].reshape(3 * boxes, 3, width)
+    near_fluid = pieces[1].reshape(3 * fluids, 3, width)
+    near_forces = pieces[2].reshape(3 * fluids, 3, width)
+    near_solid_counts = pieces[3].reshape(3, -1)[:, :boxes].reshape(-1).astype(jnp.int32)
+    near_fluid_counts = pieces[4].reshape(3, -1)[:, :fluids].reshape(-1).astype(jnp.int32)
     sf_live = jnp.sum((sf_pairs >= 0).astype(jnp.int32), axis=1)
     ss_live = jnp.sum((ss_pairs >= 0).astype(jnp.int32), axis=1)
     sf_ids = jnp.clip(sf_pairs - (me - 1) * fluids, 0, 3 * fluids - 1)
@@ -337,7 +347,7 @@
     rhs = pair_terms(
         sf_ids, sf_live, solid_counts, near_fluid_counts,
         solid_points, near_fluid, near_forces,
-        PHI_SCALE / math.sqrt(width), 0.0,
+        4, PHI_SCALE / math.sqrt(width), 0.0,
     )
     (near_rhs,) = with_halo([rhs], devices, 1)
 
@@ -345,7 +355,7 @@
         return pair_terms(
             ss_ids, ss_live, solid_counts, near_solid_counts,
             solid_points, near_solid, near.reshape(3 * boxes, 3, width),
-            PHI_SCALE / width, DIAGONAL_SHIFT, own,
+            2, PHI_SCALE / width, DIAGONAL_SHIFT, own,
         )
 
     image = operate(near_rhs, rhs)

time: 225 us -> 222 us (0.987)
  other arithmetic: 3.06 us -> 6.16 us
  Pallas kernels: 201 us -> 198 us
    pallas_call x3, Pallas kernels: 161 us -> 153 us  [pair_terms(): pl.pallas_call(functools.partial(pair_kernel, boxes, nearby, load_ids.sha...]
    pallas_call x2, Pallas kernels: 22.8 us -> 28.5 us  [with_halo(): pl.pallas_call(functools.partial(halo_kernel, devices, total), out_shape=...]
    unnamed x39 -> x28, local copies, waits for them, and re-layouts: 11 us -> 8.51 us
where the time goes in v3:
time: 222 us; the launch traced here: 221 us
  Pallas kernels  198 us (89%)
  local copies, waits for them, and re-layouts  15.9 us (7%)
  other arithmetic  6.16 us (3%)
    pallas_call x3, Pallas kernels, pair_terms(): pl.pallas_call(functools.partial(pair_kernel, boxes, nearby, load_ids.sha...  153 us
    pallas_call x2, Pallas kernels, with_halo(): pl.pallas_call(functools.partial(halo_kernel, devices, total), out_shape=...  28.5 us
    pallas_call x1, Pallas kernels, body(): pl.pallas_call(functools.partial(last_kernel, devices), out_shape=[block,...  8.54 us
    unnamed x28, local copies, waits for them, and re-layouts  8.51 us
    pallas_call x1, Pallas kernels, body(): pl.pallas_call(functools.partial(first_kernel, devices), out_shape=[jax.S...  8.47 us

profile of v3, /device:TPU:3, one launch (start us, length us, event | category | flops | bytes accessed | tf_op | source)
XLA Modules:
  0.0 221.3 jit_solution(12656548763581197306)
XLA Ops:
  0.6 0.7 convert_element_type.40
  1.3 0.7 convert_element_type.39
  2.0 0.7 add_bitcast_fusion.3
  2.9 0.8 add_bitcast_fusion.1
  4.0 0.9 copy.40.own_points
  5.0 1.0 copy.41
  6.4 0.7 copy-done.8
  7.1 12.6 %shard_map.86 = f32[3,736,128]{2,1,0:T(8,128)} custom-call(f32[736,128]{1,0:T(8,128)} %copy-done.8), custom_call_target="tpu_custom_call" | custom-call | tf_op jit(solution)/shard_map/pallas_call | solution.py:80
  19.7 0.8 slice_bitcast_fusion.1
  23.5 0.7 convert_reduce_fusion
  24.3 0.7 select_reduce_fusion
  25.5 0.7 slice-done
  26.9 61.0 %shard_map.87.refs_0_.rest_0_ = f32[24,3,256]{2,1,0:T(4,128)S(1)} custom-call(s32[864]{0:T(1024)S(1)} %reshape.289.load_ids, s32[864]{0:T(1024)S(1)} %fusion.point_ids, s32[24]{0:T(128)S(1)} %and_select_fusion.1.groups, s32[24]{0:T(128)S(1)} %copy-done.6, s32[144]{0:T(256)S(1)} %convert_element_type.42.near_counts, f32[24,3,256]{2,1,0:T(4,128)S(1)} %copy.40.own_points, ...), custom_call_target="tpu_custom_call" | custom-call | flops 566231040 | bytes 1048576 | tf_op jit(solution)/shard_map/pallas_call | solution.py:226
  88.6 15.9 %shard_map.88.rhs = f32[3,24,3,256]{3,2,1,0:T(4,128)} custom-call(f32[24,3,256]{2,1,0:T(4,128)} %copy-done.4), custom_call_target="tpu_custom_call" | custom-call | tf_op jit(solution)/shard_map/pallas_call | solution.py:80
  104.5 1.0 copy-done
  105.4 0.9 copy-done.5
  106.3 45.8 %shard_map.89.image = f32[24,3,256]{2,1,0:T(4,128)S(1)} custom-call(s32[432]{0:T(512)S(1)} %reshape.294.load_ids, s32[432]{0:T(512)S(1)} %fusion.1.point_ids, s32[24]{0:T(128)S(1)} %and_select_fusion.groups, s32[24]{0:T(128)S(1)} %copy-done.6, s32[72]{0:T(128)S(1)} %convert_element_type.47.near_counts, f32[24,3,256]{2,1,0:T(4,128)S(1)} %copy.40.own_points, ...), custom_call_target="tpu_custom_call" | custom-call | flops 283115520 | bytes 1048576 | tf_op jit(solution)/shard_map/pallas_call | solution.py:226
  152.8 8.5 %shard_map.90 = (f32[3,24,3,256]{3,2,1,0:T(4,128)}, f32[8,128]{1,0:T(8,128)}) custom-call(f32[3,24,3,256]{3,2,1,0:T(4,128)} %shard_map.88.rhs, f32[24,3,256]{2,1,0:T(4,128)} %copy-done.2), custom_call_target="tpu_custom_call" | custom-call | tf_op jit(solution)/shard_map/pallas_call | solution.py:363
  161.3 0.9 slice_bitcast_fusion.rest_0_
  162.2 1.0 copy-done.1
  163.2 45.8 %shard_map.91.second = f32[24,3,256]{2,1,0:T(4,128)S(1)} custom-call(s32[432]{0:T(512)S(1)} %reshape.294.load_ids, s32[432]{0:T(512)S(1)} %fusion.1.point_ids, s32[24]{0:T(128)S(1)} %and_select_fusion.groups, s32[24]{0:T(128)S(1)} %copy-done.6, s32[72]{0:T(128)S(1)} %convert_element_type.47.near_counts, f32[24,3,256]{2,1,0:T(4,128)S(1)} %copy.40.own_points, ...), custom_call_target="tpu_custom_call" | custom-call | flops 283115520 | bytes 1048576 | tf_op jit(solution)/shard_map/pallas_call | solution.py:226
  209.7 8.5 %shard_map.92 = (f32[24,3,256]{2,1,0:T(4,128)}, f32[24,3,256]{2,1,0:T(4,128)}) custom-call(f32[3,24,3,256]{3,2,1,0:T(4,128)} %shard_map.88.rhs, f32[24,3,256]{2,1,0:T(4,128)} %copy-done.2, f32[3,24,3,256]{3,2,1,0:T(4,128)} %get-tuple-element.28.direction, f32[24,3,256]{2,1,0:T(4,128)} %copy-done.3, f32[8,128]{1,0:T(8,128)} %get-tuple-element.29.coefs), custom_call_target="tpu_custom_call" | custom-call | tf_op jit(solution)/shard_map/pallas_call | solution.py:381
  218.2 1.5 copy.59
  219.7 1.5 copy.60
  (82 shorter events, 6.8 us)
Async XLA Ops:
  0.6 5.4 %copy-start.9 = (f32[48,3,256]{2,0,1:T(8,128)S(1)}, f32[48,3,256]{2,0,1:T(8,128)}, u32[]{:S(2)}) copy-start(f32[48,3,256]{2,0,1:T(8,128)} %param.14) | copy-start | bytes 442372
  6.4 0.8 copy-start.8
  19.7 5.7 %copy-start.7 = (f32[3,736,128]{2,1,0:T(8,128)S(1)}, f32[3,736,128]{2,1,0:T(8,128)}, u32[]{:S(2)}) copy-start(f32[3,736,128]{2,1,0:T(8,128)} %shard_map.86) | copy-start | bytes 3391492
  25.2 0.9 slice-start
  26.2 0.7 copy-start.6
  87.9 0.6 copy-start.4
  104.5 1.0 copy-start
  105.4 0.9 copy-start.5
  152.2 0.6 copy-start.2
  162.2 1.0 copy-start.1
  209.0 0.6 copy-start.3
